TPU v7x, 32 devices: a whole 2x2x4 slice. The times are simulated.
32 devices in a mesh: ctx: 16 (over z, x, core), head: 2 (over y).
Axes of the slice: x: 2, y: 2, z: 4, core: 2. Of those that a mesh axis runs over, the one named last changes fastest.
Arguments:
- tokens: bfloat16 [4096, 4096], P('ctx', 'head'), may hold values from -26 to 26
- w_query: bfloat16 [4096, 2048], P('ctx', 'head'), may hold values from -0.09375 to 0.09375, as said below
- w_key: bfloat16 [4096, 2048], P('ctx', 'head'), may hold values from -1.5 to 1.5
- w_value: bfloat16 [4096, 2048], P('ctx', 'head'), may hold values from -0.09375 to 0.09375
- w_out: bfloat16 [2048, 4096], P('head', 'ctx'), may hold values from -0.125 to 0.125
- query_down: bfloat16 [4096, 8], replicated, may hold values from -0.09375 to 0.09375
- query_up: bfloat16 [8, 2048], P(None, 'head'), may hold values from -0.5 to 0.5
- value_down: bfloat16 [4096, 8], replicated, may hold values from -0.09375 to 0.09375
- value_up: bfloat16 [8, 2048], P(None, 'head'), may hold values from -0.5 to 0.5
- shifted: int32 [16], replicated, may hold values from 0 to 1, as said below
- grad_out: bfloat16 [4096, 4096], P('ctx', 'head'), may hold values from -6 to 6
Outputs:
- output: bfloat16 [4096, 4096], P('ctx', 'head')
- grad_tokens: bfloat16 [4096, 4096], P('ctx', 'head')
- grad_query_down: float32 [4096, 8], replicated
- grad_query_up: float32 [8, 2048], P(None, 'head')
- grad_value_down: float32 [4096, 8], replicated
- grad_value_up: float32 [8, 2048], P(None, 'head')
Inputs may be any that keep to these rules, and one draw needn't show every extreme that they name: Exactly 8 of the heads are shifted. `w_query`: entries within 6 / sqrt(4096).
All inputs are finite; a program needn't handle non-finite values.
Results may differ from a plain program's by a relative error of at most 0.0095.
The roundings to bfloat16 on the way count: a program that leaves them out, or rounds other values in their place, can miss the bound.
Values may be sent and summed in bfloat16 or wider, within the bound.
A program may use at most 192 MiB of HBM per device.

v0:
```python
import jax
import jax.numpy as jnp
from jax import lax
from jax.sharding import PartitionSpec as P

HEAD_DIM = 128
G_BLOCKS = 8


def from_behind(value, axis, steps):
    count = lax.axis_size(axis)
    pairs = [(source, (source + steps) % count) for source in range(count)]
    return lax.ppermute(value, axis, pairs)


def rope(values, positions, sign):
    count = values.shape[0]
    shaped = values.reshape(count, values.shape[1] // HEAD_DIM, HEAD_DIM)
    half = HEAD_DIM // 2
    freq = jnp.power(10000.0, -jnp.arange(half, dtype=jnp.float32) * 2.0 / HEAD_DIM)
    angle = positions.astype(jnp.float32)[:, None] * freq[None, :]
    cosine = jnp.cos(angle)[:, None, :]
    sine = sign * jnp.sin(angle)[:, None, :]
    first = shaped[:, :, :half]
    second = shaped[:, :, half:]
    rotated = jnp.concatenate(
        [first * cosine - second * sine, second * cosine + first * sine], axis=2
    )
    return rotated.reshape(count, values.shape[1])


def per_device(
    tokens,
    w_query,
    w_key,
    w_value,
    w_out,
    query_down,
    query_up,
    value_down,
    value_up,
    shifted,
    grad_out,
):
    rows = tokens.shape[0]
    slice_width = tokens.shape[1]
    ctx_count = lax.axis_size("ctx")
    ctx_place = lax.axis_index("ctx")
    head_place = lax.axis_index("head")
    width_local = w_query.shape[1]
    heads_local = width_local // HEAD_DIM
    seq_total = ctx_count * rows
    group = G_BLOCKS * rows
    offset_step = group // 2
    key_rows = G_BLOCKS * rows
    scale = 1.0 / HEAD_DIM**0.5
    full_x = lax.all_gather(tokens, "head", axis=1, tiled=True)
    full32 = full_x.astype(jnp.float32)
    rinv = lax.rsqrt(jnp.mean(full32 * full32, axis=-1, keepdims=True) + 1e-05)
    xn = full32 * rinv
    normed = xn.astype(jnp.bfloat16)
    low_q = jnp.dot(normed, query_down, preferred_element_type=jnp.float32).astype(jnp.bfloat16)
    low_v = jnp.dot(normed, value_down, preferred_element_type=jnp.float32).astype(jnp.bfloat16)
    stacked = jnp.stack([w_query, w_key, w_value])
    whole = lax.all_gather(stacked, "ctx", axis=1, tiled=True)
    q_lin = jnp.dot(normed, whole[0], preferred_element_type=jnp.float32)
    k_lin = jnp.dot(normed, whole[1], preferred_element_type=jnp.float32)
    v_lin = jnp.dot(normed, whole[2], preferred_element_type=jnp.float32)
    out_weight = lax.all_gather(w_out, "ctx", axis=1, tiled=True)
    positions = ctx_place * rows + jnp.arange(rows, dtype=jnp.int32)
    query = rope(
        q_lin + 2.0 * jnp.dot(low_q, query_up, preferred_element_type=jnp.float32), positions, 1.0
    ).astype(jnp.bfloat16)
    key = rope(k_lin, positions, 1.0).astype(jnp.bfloat16)
    value = (v_lin + 2.0 * jnp.dot(low_v, value_up, preferred_element_type=jnp.float32)).astype(
        jnp.bfloat16
    )
    keyval = jnp.stack([key, value])
    blocks = [keyval]
    for step in range(1, G_BLOCKS):
        blocks.append(from_behind(keyval, "ctx", step))
    all_keyval = jnp.concatenate(blocks, axis=1)
    sources = jnp.mod(ctx_place - jnp.arange(G_BLOCKS, dtype=jnp.int32), ctx_count)
    key_pos = (sources[:, None] * rows + jnp.arange(rows, dtype=jnp.int32)[None, :]).reshape(
        key_rows
    )
    offsets = lax.dynamic_slice_in_dim(shifted, head_place * heads_local, heads_local) * offset_step
    query_c = jnp.mod(positions[None, :] - offsets[:, None], seq_total)
    key_c = jnp.mod(key_pos[None, :] - offsets[:, None], seq_total)
    allowed = jnp.logical_and(
        (query_c // group)[:, :, None] == (key_c // group)[:, None, :],
        key_c[:, None, :] <= query_c[:, :, None],
    )
    query_h = query.reshape(rows, heads_local, HEAD_DIM)
    key_h = all_keyval[0].reshape(key_rows, heads_local, HEAD_DIM)
    value_h = all_keyval[1].reshape(key_rows, heads_local, HEAD_DIM)
    scores = jnp.einsum("qhd,khd->hqk", query_h, key_h, preferred_element_type=jnp.float32) * scale
    scores = jnp.where(allowed, scores, -jnp.inf)
    top = jnp.max(scores, axis=-1, keepdims=True)
    expo = jnp.exp(scores - top)
    prob32 = expo / jnp.sum(expo, axis=-1, keepdims=True)
    prob = prob32.astype(jnp.bfloat16)
    context = jnp.einsum("hqk,khd->qhd", prob, value_h, preferred_element_type=jnp.float32)
    context = context.reshape(rows, width_local).astype(jnp.bfloat16)
    partial_value = jnp.dot(context, out_weight, preferred_element_type=jnp.float32)
    attn = lax.psum_scatter(partial_value, "head", scatter_dimension=1, tiled=True)
    output = (tokens.astype(jnp.float32) + attn).astype(jnp.bfloat16)
    full_dy = lax.all_gather(grad_out, "head", axis=1, tiled=True)
    d_context = jnp.dot(full_dy, out_weight.T, preferred_element_type=jnp.float32).astype(
        jnp.bfloat16
    )
    dctx_h = d_context.reshape(rows, heads_local, HEAD_DIM)
    dprob = jnp.einsum("qhd,khd->hqk", dctx_h, value_h, preferred_element_type=jnp.float32)
    delta = jnp.sum(prob32 * dprob, axis=-1, keepdims=True)
    dscore = (prob32 * (dprob - delta) * scale).astype(jnp.bfloat16)
    grad_q = jnp.einsum("hqk,khd->qhd", dscore, key_h, preferred_element_type=jnp.float32)
    grad_k = jnp.einsum("hqk,qhd->khd", dscore, query_h, preferred_element_type=jnp.float32)
    grad_v = jnp.einsum("hqk,qhd->khd", prob, dctx_h, preferred_element_type=jnp.float32)
    terms = jnp.stack(
        [grad_k.reshape(G_BLOCKS, rows, width_local), grad_v.reshape(G_BLOCKS, rows, width_local)],
        axis=1,
    )
    summed = terms[0]
    for step in range(1, G_BLOCKS):
        summed = summed + from_behind(terms[step].astype(jnp.bfloat16), "ctx", -step).astype(
            jnp.float32
        )
    dq_pre = rope(grad_q.reshape(rows, width_local), positions, -1.0).astype(jnp.bfloat16)
    dk_pre = rope(summed[0], positions, -1.0).astype(jnp.bfloat16)
    dv_b = summed[1].astype(jnp.bfloat16)
    d_normed = jnp.dot(dq_pre, whole[0].T, preferred_element_type=jnp.float32)
    d_normed = d_normed + jnp.dot(dk_pre, whole[1].T, preferred_element_type=jnp.float32)
    d_normed = d_normed + jnp.dot(dv_b, whole[2].T, preferred_element_type=jnp.float32)
    g_q = jnp.dot(dq_pre, query_up.T, preferred_element_type=jnp.float32)
    g_v = jnp.dot(dv_b, value_up.T, preferred_element_type=jnp.float32)
    d_normed = d_normed + 2.0 * jnp.dot(
        g_q, query_down.astype(jnp.float32).T, precision=lax.Precision.HIGHEST
    )
    d_normed = d_normed + 2.0 * jnp.dot(
        g_v, value_down.astype(jnp.float32).T, precision=lax.Precision.HIGHEST
    )
    x_slice = lax.dynamic_slice_in_dim(xn, head_place * slice_width, slice_width, 1)
    mine = lax.psum_scatter(d_normed, "head", scatter_dimension=1, tiled=True)
    row_sum = lax.psum(jnp.sum(mine * x_slice, axis=-1, keepdims=True), "head")
    row_mean = row_sum / full_x.shape[1]
    grad_tokens = (grad_out.astype(jnp.float32) + rinv * (mine - x_slice * row_mean)).astype(
        jnp.bfloat16
    )
    scale_out = 1.0 / seq_total**0.5
    normed32 = normed.astype(jnp.float32)
    down_q = 2.0 * jnp.dot(normed32.T, g_q, precision=lax.Precision.HIGHEST)
    down_v = 2.0 * jnp.dot(normed32.T, g_v, precision=lax.Precision.HIGHEST)
    up_q = 2.0 * jnp.dot(low_q.T, dq_pre, preferred_element_type=jnp.float32)
    up_v = 2.0 * jnp.dot(low_v.T, dv_b, preferred_element_type=jnp.float32)
    down_q, down_v = lax.psum((down_q, down_v), ("ctx", "head"))
    up_q, up_v = lax.psum((up_q, up_v), "ctx")
    return (
        output,
        grad_tokens,
        down_q * scale_out,
        up_q * scale_out,
        down_v * scale_out,
        up_v * scale_out,
    )


def solution(mesh):
    in_specs = (
        P("ctx", "head"),
        P("ctx", "head"),
        P("ctx", "head"),
        P("ctx", "head"),
        P("head", "ctx"),
        P(),
        P(None, "head"),
        P(),
        P(None, "head"),
        P(),
        P("ctx", "head"),
    )
    out_specs = (P("ctx", "head"), P("ctx", "head"), P(), P(None, "head"), P(), P(None, "head"))
    return jax.shard_map(
        per_device, mesh=mesh, in_specs=in_specs, out_specs=out_specs, check_vma=False
    )
```

profile of v0, /device:TPU:0, one launch (start us, length us, event | category | flops | bytes accessed | tf_op | source)
XLA Modules:
  0.0 1152.3 jit_solution(5949515302681027285)
XLA Ops:
  13.6 31.8 %all-gather.5.cloned.1.call-done = bf16[256,4096]{1,0:T(8,128)(2,1)} async-done(((bf16[256,2048]{1,0:T(8,128)(2,1)}), bf16[256,4096]{1,0:T(8,128)(2,1)}) %all-gather.5.cloned.1.call-update) | async-done | bytes 2097168 | tf_op jit(solution)/shard_map/all_gather | solution.py:57
  50.7 124.8 %all-gather.7.cloned.1.call-done = bf16[3,4096,1024]{2,1,0:T(8,128)(2,1)} async-done(((bf16[3,256,1024]{2,1,0:T(8,128)(2,1)}), bf16[3,4096,1024]{2,1,0:T(8,128)(2,1)}) %all-gather.7.cloned.1.call-update) | async-done | bytes 25165840 | tf_op jit(solution)/shard_map/all_gather | solution.py:65
  184.3 8.1 slice_bitcast_fusion.6
  192.4 11.3 copy.29
  226.0 36.8 %collective-permute-done.1 = bf16[2,256,1024]{2,1,0:T(8,128)(2,1)S(1)} collective-permute-done((bf16[2,256,1024]{2,1,0:T(8,128)(2,1)S(1)}, bf16[2,256,1024]{2,1,0:T(8,128)(2,1)S(1)}, u32[]{:S(2)}, u32[]{:S(2)}) %collective-permute-start.1) | collective-permute-done | bytes 1048608 | tf_op jit(solution)/shard_map/ppermute | solution.py:13
  264.1 21.2 %collective-permute-done = bf16[2,256,1024]{2,1,0:T(8,128)(2,1)} collective-permute-done((bf16[2,256,1024]{2,1,0:T(8,128)(2,1)S(1)}, bf16[2,256,1024]{2,1,0:T(8,128)(2,1)}, u32[]{:S(2)}, u32[]{:S(2)}) %collective-permute-start) | collective-permute-done | bytes 1048608 | tf_op jit(solution)/shard_map/ppermute | solution.py:13
  285.5 161.1 %all-gather.9.cloned.1.call-done = bf16[1024,4096]{1,0:T(8,128)(2,1)} async-done(((bf16[1024,256]{1,0:T(8,128)(2,1)}), bf16[1024,4096]{1,0:T(8,128)(2,1)}) %all-gather.9.cloned.1.call-update) | async-done | bytes 8388624 | tf_op jit(solution)/shard_map/all_gather | solution.py:69
  479.1 6.6 copy.42
  490.9 11.8 %fusion.94 = (f32[8,256]{1,0:T(8,128)S(1)}, f32[8,256,2048]{2,1,0:T(8,128)}) fusion(s32[8,256]{1,0:T(8,128)S(1)} %get-tuple-element.37, s32[8,2048]{1,0:T(8,128)S(1)} %copy-done.23, s32[8,2048]{1,0:T(8,128)S(1)} %get-tuple-element.31, s32[8,256]{1,0:T(8,128)S(1)} %get-tuple-element.36, bf16[2048,8,128]{0,2,1:T(8,128)(2,1)} %bitcast.138, ...), kind=kOutput, calls=%fused_computation.165 | convolution fusion | flops 1104152576 | bytes 21651456 | tf_op jit(solution)/shard_map/sub | solution.py:100
  502.7 7.0 fusion.32
  509.7 7.5 copy.47
  517.2 8.2 fusion.37
  525.4 26.5 %fusion.6 = f32[8,128,2048]{2,1,0:T(8,128)} fusion(f32[8,256,2048]{2,1,0:T(8,128)} %fusion.37, bf16[256,8,64]{0,2,1:T(8,128)(2,1)S(1)} %copy-done.15, bf16[256,8,64]{0,2,1:T(8,128)(2,1)S(1)} %get-tuple-element.23, f32[8,256,2048]{2,1,0:T(8,128)} %get-tuple-element.39, f32[8,256]{1,0:T(8,128)S(1)} %get-tuple-element.38), kind=kOutput, calls=%fused_computation.7 | convolution fusion | flops 1104154624 | bytes 42475520 | tf_op jit(solution)/shard_map/hqk,qhd->khd/dot_general | solution.py:117
  551.9 10.8 copy.46
  568.8 6.6 copy_dynamic-update-slice_fusion
  595.7 11.0 fusion.53
  611.9 29.0 %fusion.48 = f32[256,8,128]{0,2,1:T(8,128)} fusion(bf16[2048,8,128]{0,2,1:T(8,128)(2,1)} %bitcast.139, f32[8,256,2048]{2,1,0:T(8,128)} %fusion.37, f32[8,256,2048]{2,1,0:T(8,128)} %get-tuple-element.39, f32[8,256]{1,0:T(8,128)} %copy-done.32), kind=kOutput, calls=%fused_computation.64 | convolution fusion | flops 1103106048 | bytes 38805504 | tf_op jit(solution)/shard_map/hqk,khd->qhd/dot_general | solution.py:116
  642.0 113.5 %collective-permute-start.8 = (bf16[2,256,1024]{1,2,0:T(8,128)(2,1)S(1)}, bf16[2,256,1024]{1,2,0:T(8,128)(2,1)S(1)}, u32[]{:S(2)}, u32[]{:S(2)}) collective-permute-start(bf16[2,256,1024]{1,2,0:T(8,128)(2,1)S(1)} %get-tuple-element.16), channel_id=1, source_target_pairs={{0,28},{2,30},{4,0},{6,2},{8,4},{10,6},{12,8},{14,10},{16,12},{18,... | collective-permute-start | bytes 3145736 | tf_op jit(solution)/shard_map/ppermute | solution.py:13
  760.3 7.5 collective-permute-done.8
  776.1 7.8 fusion.95
  812.0 75.7 %all-reduce.7.cloned.1.call-done = (f32[8,1024]{1,0:T(8,128)}, f32[8,1024]{1,0:T(8,128)}) async-done(((f32[8,1024]{1,0:T(8,128)}, f32[8,1024]{1,0:T(8,128)}), (f32[8,1024]{1,0:T(8,128)}, f32[8,1024]{1,0:T(8,128)})) %all-reduce.7.cloned.1.call-update) | async-done | bytes 65552 | tf_op jit(solution)/shard_map/psum | solution.py:156
  890.4 131.2 %all-reduce.5.cloned.1.call-done = (f32[4096,8]{0,1:T(8,128)}, f32[4096,8]{0,1:T(8,128)}) async-done(((f32[4096,8]{0,1:T(8,128)}, f32[4096,8]{0,1:T(8,128)}), (f32[4096,8]{0,1:T(8,128)}, f32[4096,8]{0,1:T(8,128)})) %all-reduce.5.cloned.1.call-update) | async-done | bytes 262160 | tf_op jit(solution)/shard_map/psum | solution.py:155
  1024.8 52.6 %reduce-scatter.3.cloned.1.call-done = f32[256,2048]{1,0:T(8,128)} async-done(((f32[256,4096]{1,0:T(8,128)}), f32[256,2048]{1,0:T(8,128)}) %reduce-scatter.3.cloned.1.call-update) | async-done | bytes 2097168 | tf_op jit(solution)/shard_map/reduce_scatter | solution.py:106
  1080.2 53.8 %reduce-scatter.5.cloned.1.call-done = f32[256,2048]{1,0:T(8,128)} async-done(((f32[256,4096]{1,0:T(8,128)}), f32[256,2048]{1,0:T(8,128)}) %reduce-scatter.5.cloned.1.call-update) | async-done | bytes 2097168 | tf_op jit(solution)/shard_map/reduce_scatter | solution.py:143
  (173 shorter events, 174.9 us)
Async XLA Ops:
  7.2 38.2 %all-gather.5.cloned.1.call-start = ((), (), s32[]{:S(2)}) async-start(), calls=%async_computation.2 | async-start | bytes 3145728 | tf_op jit(solution)/shard_map/all_gather | solution.py:57
  7.9 167.6 %all-gather.7.cloned.1.call-start = ((), (), s32[]{:S(2)}) async-start(), calls=%async_computation.3 | async-start | bytes 26738688 | tf_op jit(solution)/shard_map/all_gather | solution.py:65
  10.7 274.8 %all-gather.11.cloned.1.call-start = ((), (), s32[]{:S(2)}) async-start(), calls=%async_computation.6 | async-start | bytes 3145728 | tf_op jit(solution)/shard_map/all_gather | solution.py:108
  11.5 435.2 %all-gather.9.cloned.1.call-start = ((), (), s32[]{:S(2)}) async-start(), calls=%async_computation.4 | async-start | bytes 8912896 | tf_op jit(solution)/shard_map/all_gather | solution.py:69
  12.0 875.6 %all-reduce.7.cloned.1.call-start = ((), (), s32[]{:S(2)}) async-start(), calls=%async_computation.9 | async-start | bytes 131072 | tf_op jit(solution)/shard_map/psum | solution.py:156
  13.6 196.0 %copy-start.11 = (f32[256,64]{0,1:T(8,128)}, f32[256,64]{0,1:T(8,128)S(1)}, u32[]{:S(2)}) copy-start(f32[256,64]{0,1:T(8,128)S(1)} %get-tuple-element.35) | copy-start | bytes 196612
  218.3 44.5 %collective-permute-start.1 = (bf16[2,256,1024]{2,1,0:T(8,128)(2,1)S(1)}, bf16[2,256,1024]{2,1,0:T(8,128)(2,1)S(1)}, u32[]{:S(2)}, u32[]{:S(2)}) collective-permute-start(bf16[2,256,1024]{2,1,0:T(8,128)(2,1)S(1)} %get-tuple-element.27), channel_id=1, source_target_pairs={{0,4},{2,6},{4,8},{6,10},{8,12},{10,14},{12,16},{14,18},{16,20},{1... | collective-permute-start | bytes 3145736 | tf_op jit(solution)/shard_map/ppermute | solution.py:13
  219.7 65.6 %collective-permute-start = (bf16[2,256,1024]{2,1,0:T(8,128)(2,1)S(1)}, bf16[2,256,1024]{2,1,0:T(8,128)(2,1)}, u32[]{:S(2)}, u32[]{:S(2)}) collective-permute-start(bf16[2,256,1024]{2,1,0:T(8,128)(2,1)S(1)} %get-tuple-element.27), channel_id=1, source_target_pairs={{0,2},{2,4},{4,6},{6,8},{8,10},{10,12},{12,14},{14,16},{16,18},{18... | collective-permute-start | bytes 3145736 | tf_op jit(solution)/shard_map/ppermute | solution.py:13
  220.7 235.9 %collective-permute-start.2 = (bf16[2,256,1024]{2,1,0:T(8,128)(2,1)S(1)}, bf16[2,256,1024]{2,1,0:T(8,128)(2,1)}, u32[]{:S(2)}, u32[]{:S(2)}) collective-permute-start(bf16[2,256,1024]{2,1,0:T(8,128)(2,1)S(1)} %get-tuple-element.27), channel_id=1, source_target_pairs={{0,6},{2,8},{4,10},{6,12},{8,14},{10,16},{12,18},{14,20},{16,22},{... | collective-permute-start | bytes 3145736 | tf_op jit(solution)/shard_map/ppermute | solution.py:13
  223.4 244.6 %collective-permute-start.5 = (bf16[2,256,1024]{2,1,0:T(8,128)(2,1)S(1)}, bf16[2,256,1024]{2,1,0:T(8,128)(2,1)}, u32[]{:S(2)}, u32[]{:S(2)}) collective-permute-start(bf16[2,256,1024]{2,1,0:T(8,128)(2,1)S(1)} %get-tuple-element.27), channel_id=1, source_target_pairs={{0,12},{2,14},{4,16},{6,18},{8,20},{10,22},{12,24},{14,26},{16,28}... | collective-permute-start | bytes 3145736 | tf_op jit(solution)/shard_map/ppermute | solution.py:13
  226.0 239.7 %collective-permute-start.4 = (bf16[2,256,1024]{2,1,0:T(8,128)(2,1)S(1)}, bf16[2,256,1024]{2,1,0:T(8,128)(2,1)}, u32[]{:S(2)}, u32[]{:S(2)}) collective-permute-start(bf16[2,256,1024]{2,1,0:T(8,128)(2,1)S(1)} %get-tuple-element.27), channel_id=1, source_target_pairs={{0,10},{2,12},{4,14},{6,16},{8,18},{10,20},{12,22},{14,24},{16,26}... | collective-permute-start | bytes 3145736 | tf_op jit(solution)/shard_map/ppermute | solution.py:13
  262.8 196.0 %collective-permute-start.3 = (bf16[2,256,1024]{2,1,0:T(8,128)(2,1)S(1)}, bf16[2,256,1024]{2,1,0:T(8,128)(2,1)}, u32[]{:S(2)}, u32[]{:S(2)}) collective-permute-start(bf16[2,256,1024]{2,1,0:T(8,128)(2,1)S(1)} %get-tuple-element.27), channel_id=1, source_target_pairs={{0,8},{2,10},{4,12},{6,14},{8,16},{10,18},{12,20},{14,22},{16,24},... | collective-permute-start | bytes 3145736 | tf_op jit(solution)/shard_map/ppermute | solution.py:13
  285.3 185.0 %collective-permute-start.6 = (bf16[2,256,1024]{2,1,0:T(8,128)(2,1)S(1)}, bf16[2,256,1024]{2,1,0:T(8,128)(2,1)}, u32[]{:S(2)}, u32[]{:S(2)}) collective-permute-start(bf16[2,256,1024]{2,1,0:T(8,128)(2,1)S(1)} %get-tuple-element.27), channel_id=1, source_target_pairs={{0,14},{2,16},{4,18},{6,20},{8,22},{10,24},{12,26},{14,28},{16,30}... | collective-permute-start | bytes 3145736 | tf_op jit(solution)/shard_map/ppermute | solution.py:13
  589.5 51.3 %collective-permute-start.7 = (bf16[2,256,1024]{1,2,0:T(8,128)(2,1)}, bf16[2,256,1024]{1,2,0:T(8,128)(2,1)}, u32[]{:S(2)}, u32[]{:S(2)}) collective-permute-start(bf16[2,256,1024]{1,2,0:T(8,128)(2,1)} %get-tuple-element.10), channel_id=1, source_target_pairs={{0,30},{2,0},{4,2},{6,4},{8,6},{10,8},{12,10},{14,12},{16,14},{18,... | collective-permute-start | bytes 3145736 | tf_op jit(solution)/shard_map/ppermute | solution.py:13
  595.5 46.4 %collective-permute-start.13 = (bf16[2,256,1024]{1,2,0:T(8,128)(2,1)}, bf16[2,256,1024]{1,2,0:T(8,128)(2,1)}, u32[]{:S(2)}, u32[]{:S(2)}) collective-permute-start(bf16[2,256,1024]{1,2,0:T(8,128)(2,1)} %get-tuple-element.11), channel_id=1, source_target_pairs={{0,18},{2,20},{4,22},{6,24},{8,26},{10,28},{12,30},{14,0},{16,2},{... | collective-permute-start | bytes 3145736 | tf_op jit(solution)/shard_map/ppermute | solution.py:13
  606.7 153.6 %collective-permute-start.12 = (bf16[2,256,1024]{1,2,0:T(8,128)(2,1)}, bf16[2,256,1024]{1,2,0:T(8,128)(2,1)}, u32[]{:S(2)}, u32[]{:S(2)}) collective-permute-start(bf16[2,256,1024]{1,2,0:T(8,128)(2,1)} %get-tuple-element.12), channel_id=1, source_target_pairs={{0,20},{2,22},{4,24},{6,26},{8,28},{10,30},{12,0},{14,2},{16,4},{1... | collective-permute-start | bytes 3145736 | tf_op jit(solution)/shard_map/ppermute | solution.py:13
  610.4 149.9 %collective-permute-start.11 = (bf16[2,256,1024]{1,2,0:T(8,128)(2,1)}, bf16[2,256,1024]{1,2,0:T(8,128)(2,1)}, u32[]{:S(2)}, u32[]{:S(2)}) collective-permute-start(bf16[2,256,1024]{1,2,0:T(8,128)(2,1)} %get-tuple-element.13), channel_id=1, source_target_pairs={{0,22},{2,24},{4,26},{6,28},{8,30},{10,0},{12,2},{14,4},{16,6},{18... | collective-permute-start | bytes 3145736 | tf_op jit(solution)/shard_map/ppermute | solution.py:13
  611.2 149.2 %collective-permute-start.10 = (bf16[2,256,1024]{1,2,0:T(8,128)(2,1)}, bf16[2,256,1024]{1,2,0:T(8,128)(2,1)}, u32[]{:S(2)}, u32[]{:S(2)}) collective-permute-start(bf16[2,256,1024]{1,2,0:T(8,128)(2,1)} %get-tuple-element.14), channel_id=1, source_target_pairs={{0,24},{2,26},{4,28},{6,30},{8,0},{10,2},{12,4},{14,6},{16,8},{18,... | collective-permute-start | bytes 3145736 | tf_op jit(solution)/shard_map/ppermute | solution.py:13
  640.9 119.4 %collective-permute-start.9 = (bf16[2,256,1024]{1,2,0:T(8,128)(2,1)}, bf16[2,256,1024]{1,2,0:T(8,128)(2,1)S(1)}, u32[]{:S(2)}, u32[]{:S(2)}) collective-permute-start(bf16[2,256,1024]{1,2,0:T(8,128)(2,1)} %get-tuple-element.15), channel_id=1, source_target_pairs={{0,26},{2,28},{4,30},{6,0},{8,2},{10,4},{12,6},{14,8},{16,10},{18,... | collective-permute-start | bytes 3145736 | tf_op jit(solution)/shard_map/ppermute | solution.py:13
  642.0 125.9 %collective-permute-start.8 = (bf16[2,256,1024]{1,2,0:T(8,128)(2,1)S(1)}, bf16[2,256,1024]{1,2,0:T(8,128)(2,1)S(1)}, u32[]{:S(2)}, u32[]{:S(2)}) collective-permute-start(bf16[2,256,1024]{1,2,0:T(8,128)(2,1)S(1)} %get-tuple-element.16), channel_id=1, source_target_pairs={{0,28},{2,30},{4,0},{6,2},{8,4},{10,6},{12,8},{14,10},{16,12},{18,... | collective-permute-start | bytes 3145736 | tf_op jit(solution)/shard_map/ppermute | solution.py:13
  774.2 247.4 %all-reduce.5.cloned.1.call-start = ((), (), s32[]{:S(2)}) async-start(), calls=%async_computation.8 | async-start | bytes 524288 | tf_op jit(solution)/shard_map/psum | solution.py:155
  776.0 301.4 %reduce-scatter.3.cloned.1.call-start = ((), (), s32[]{:S(2)}) async-start(), calls=%async_computation.5 | async-start | bytes 6291456 | tf_op jit(solution)/shard_map/reduce_scatter | solution.py:106
  783.9 350.1 %reduce-scatter.5.cloned.1.call-start = ((), (), s32[]{:S(2)}) async-start(), calls=%async_computation.7 | async-start | bytes 6291456 | tf_op jit(solution)/shard_map/reduce_scatter | solution.py:143
  809.4 267.9 %copy-start.10 = (bf16[256,2048]{1,0:T(8,128)(2,1)S(1)}, bf16[256,2048]{1,0:T(8,128)(2,1)}, u32[]{:S(2)}) copy-start(bf16[256,2048]{1,0:T(8,128)(2,1)} %param.11) | copy-start | bytes 3145732
  (32 other events, 1748.7 us)
Sparse Core Ops, SparseCore 0:
  9.6 35.8 all-gather.4
  47.0 128.5 all-gather.6
  177.1 33.1 all-gather.10
  212.3 234.3 all-gather.8
  774.3 113.3 all-reduce.6
  894.7 126.8 all-reduce.4
  1024.0 53.2 reduce-scatter.2
  1079.6 54.3 reduce-scatter.4
where the time goes:
time: 1160 us; the launch traced here: 1150 us
  waiting for transfers between devices  704 us (61%)
  matrix products  159 us (14%)
  starting transfers between devices  134 us (12%)
  local copies, waits for them, and re-layouts  97.5 us (8%)
  other arithmetic  37.6 us (3%)
  between operations  15.1 us (1%)
    all_gather x1, waiting for transfers between devices, per_device(): out_weight = lax.all_gather(w_out, 'ctx', axis=1, tiled=True)  161 us
    ppermute x14, starting transfers between devices, from_behind(): return lax.ppermute(value, axis, pairs)  134 us
    psum x1, waiting for transfers between devices, per_device(): down_q, down_v = lax.psum((down_q, down_v), ('ctx', 'head'))  131 us
    all_gather x1, waiting for transfers between devices, per_device(): whole = lax.all_gather(stacked, 'ctx', axis=1, tiled=True)  125 us
    psum x1, waiting for transfers between devices, per_device(): up_q, up_v = lax.psum((up_q, up_v), 'ctx')  75.7 us
    ppermute x14, waiting for transfers between devices, from_behind(): return lax.ppermute(value, axis, pairs)  70.6 us
    reduce_scatter x1, waiting for transfers between devices, per_device(): mine = lax.psum_scatter(d_normed, 'head', scatter_dimension=1, tiled=True)  53.8 us
    reduce_scatter x1, waiting for transfers between devices, per_device(): lax.psum_scatter(partial_value, 'head', scatter_dimension=1, tiled=True)  52.6 us
  transfers between devices with their start and end apart: 22, of which 12 were waited for; matrix products, arithmetic and copies ran while one was open for 14% of the time, Pallas kernels for 0%

commit v1 on v0

v1 whole, which is shorter than its diff:
```python
import functools

import jax
import jax.numpy as jnp
from jax import lax
from jax.experimental import pallas as pl
from jax.experimental.pallas import tpu as pltpu
from jax.sharding import PartitionSpec as P

HEAD_DIM = 128
G_BLOCKS = 8
LAST = (((1,), (1,)), ((), ()))
FIRST = (((0,), (0,)), ((), ()))


def angles(positions):
    half = HEAD_DIM // 2
    freq = jnp.power(10000.0, -jnp.arange(half, dtype=jnp.float32) * 2.0 / HEAD_DIM)
    angle = positions.astype(jnp.float32)[:, None] * freq[None, :]
    return jnp.cos(angle), jnp.sin(angle)


def rope(values, cosine, sine):
    count = values.shape[0]
    shaped = values.reshape(count, values.shape[1] // HEAD_DIM, HEAD_DIM)
    half = HEAD_DIM // 2
    cosine = cosine[:, None, :]
    sine = sine[:, None, :]
    first = shaped[:, :, :half]
    second = shaped[:, :, half:]
    rotated = jnp.concatenate(
        [first * cosine - second * sine, second * cosine + first * sine], axis=2
    )
    return rotated.reshape(count, values.shape[1])


def swapped(value):
    return lax.ppermute(value, "head", [(0, 1), (1, 0)])


def gather_head(value):
    if lax.axis_size("head") != 2:
        return lax.all_gather(value, "head", axis=1, tiled=True)
    other = swapped(value)
    first = lax.axis_index("head") == 0
    left = jnp.where(first, value, other)
    right = jnp.where(first, other, value)
    return jnp.concatenate([left, right], axis=1)


def scatter_head(value):
    if lax.axis_size("head") != 2:
        return lax.psum_scatter(value, "head", scatter_dimension=1, tiled=True)
    place = lax.axis_index("head")
    width = value.shape[1] // 2
    theirs = lax.dynamic_slice_in_dim(value, (1 - place) * width, width, 1)
    mine = lax.dynamic_slice_in_dim(value, place * width, width, 1)
    return mine + swapped(theirs.astype(jnp.bfloat16)).astype(jnp.float32)


def sum_head(value):
    if lax.axis_size("head") != 2:
        return lax.psum(value, "head")
    return value + swapped(value)


def attend_kernel(block, q_ref, k_ref, v_ref, g_ref, cos_ref, sin_ref, out_ref, dk_acc, dv_acc):
    count = q_ref.shape[0]
    scale = 1.0 / HEAD_DIM**0.5
    dk_acc[...] = jnp.zeros_like(dk_acc)
    dv_acc[...] = jnp.zeros_like(dv_acc)

    def unrope(values, rows):
        turned = pltpu.roll(values, HEAD_DIM // 2, 1)
        return (values * cos_ref[rows, :] + turned * sin_ref[rows, :]).astype(jnp.bfloat16)

    for step in range(count // block):
        rows = slice(step * block, (step + 1) * block)
        seen = slice(0, (step + 1) * block)
        q = q_ref[rows, :]
        g = g_ref[rows, :]
        k = k_ref[seen, :]
        v = v_ref[seen, :]
        scores = lax.dot_general(q, k, LAST, preferred_element_type=jnp.float32) * scale
        q_place = step * block + lax.broadcasted_iota(jnp.int32, scores.shape, 0)
        k_place = lax.broadcasted_iota(jnp.int32, scores.shape, 1)
        scores = jnp.where(k_place <= q_place, scores, -jnp.inf)
        expo = jnp.exp(scores - jnp.max(scores, axis=-1, keepdims=True))
        prob32 = expo * (1.0 / jnp.sum(expo, axis=-1, keepdims=True))
        prob = prob32.astype(jnp.bfloat16)
        out_ref[0, rows, :] = jnp.dot(prob, v, preferred_element_type=jnp.float32).astype(
            jnp.bfloat16
        )
        dprob = lax.dot_general(g, v, LAST, preferred_element_type=jnp.float32)
        delta = jnp.sum(prob32 * dprob, axis=-1, keepdims=True)
        dscore = (prob32 * (dprob - delta) * scale).astype(jnp.bfloat16)
        out_ref[1, rows, :] = unrope(jnp.dot(dscore, k, preferred_element_type=jnp.float32), rows)
        dk_acc[seen, :] += lax.dot_general(dscore, q, FIRST, preferred_element_type=jnp.float32)
        dv_acc[seen, :] += lax.dot_general(prob, g, FIRST, preferred_element_type=jnp.float32)
    out_ref[2, :, :] = unrope(dk_acc[...], slice(0, count))
    out_ref[3, :, :] = dv_acc[...].astype(jnp.bfloat16)


def attend(query, key, value, d_context, cosine, sine):
    count = query.shape[0]
    return pl.pallas_call(
        functools.partial(attend_kernel, 256),
        out_shape=jax.ShapeDtypeStruct((4, count, HEAD_DIM), jnp.bfloat16),
        in_specs=[pl.BlockSpec(memory_space=pltpu.VMEM)] * 6,
        out_specs=pl.BlockSpec(memory_space=pltpu.VMEM),
        scratch_shapes=[
            pltpu.VMEM((count, HEAD_DIM), jnp.float32),
            pltpu.VMEM((count, HEAD_DIM), jnp.float32),
        ],
        compiler_params=pltpu.CompilerParams(vmem_limit_bytes=48 * 1024 * 1024),
        cost_estimate=pl.CostEstimate(
            flops=10 * count * count * HEAD_DIM // 2,
            bytes_accessed=16 * count * HEAD_DIM * 2,
            transcendentals=count * count // 2,
        ),
    )(query, key, value, d_context, cosine, sine)


def per_device(
    tokens,
    w_query,
    w_key,
    w_value,
    w_out,
    query_down,
    query_up,
    value_down,
    value_up,
    shifted,
    grad_out,
):
    rows = tokens.shape[0]
    slice_width = tokens.shape[1]
    ctx_count = lax.axis_size("ctx")
    ctx_place = lax.axis_index("ctx")
    head_count = lax.axis_size("head")
    head_place = lax.axis_index("head")
    width_local = w_query.shape[1]
    heads_local = width_local // HEAD_DIM
    seq_total = ctx_count * rows
    group = G_BLOCKS * rows
    groups = ctx_count // G_BLOCKS
    items = heads_local * groups
    assert items <= ctx_count
    half_group = G_BLOCKS // 2
    rank = query_down.shape[1]

    whole = [
        lax.all_gather(w, "ctx", axis=0, tiled=True) for w in (w_query, w_key, w_value, w_out.T)
    ]

    full_x = gather_head(tokens)
    full_dy = gather_head(grad_out)
    full32 = full_x.astype(jnp.float32)
    rinv = lax.rsqrt(jnp.mean(full32 * full32, axis=-1, keepdims=True) + 1e-05)
    xn = full32 * rinv
    normed = xn.astype(jnp.bfloat16)
    low_q = jnp.dot(normed, query_down, preferred_element_type=jnp.float32).astype(jnp.bfloat16)
    low_v = jnp.dot(normed, value_down, preferred_element_type=jnp.float32).astype(jnp.bfloat16)
    positions = ctx_place * rows + jnp.arange(rows, dtype=jnp.int32)
    cosine, sine = angles(positions)
    q_lin = jnp.dot(normed, whole[0], preferred_element_type=jnp.float32)
    k_lin = jnp.dot(normed, whole[1], preferred_element_type=jnp.float32)
    v_lin = jnp.dot(normed, whole[2], preferred_element_type=jnp.float32)
    query = rope(
        q_lin + 2.0 * jnp.dot(low_q, query_up, preferred_element_type=jnp.float32), cosine, sine
    ).astype(jnp.bfloat16)
    key = rope(k_lin, cosine, sine).astype(jnp.bfloat16)
    value = (v_lin + 2.0 * jnp.dot(low_v, value_up, preferred_element_type=jnp.float32)).astype(
        jnp.bfloat16
    )
    d_context = jnp.dot(full_dy, whole[3], preferred_element_type=jnp.float32).astype(jnp.bfloat16)

    local_shift = lax.dynamic_slice_in_dim(shifted, head_place * heads_local, heads_local)
    item = jnp.minimum(ctx_place, items - 1)
    item_group = item % groups
    item_shift = lax.dynamic_index_in_dim(local_shift, item // groups, keepdims=False)
    start = (item_group * G_BLOCKS + item_shift * half_group) % ctx_count

    packed = jnp.stack([query, key, value, d_context])
    packed = packed.reshape(4, rows, heads_local, HEAD_DIM).transpose(2, 0, 1, 3)
    packed = jnp.broadcast_to(
        packed[:, None], (heads_local, groups, 4, rows, HEAD_DIM)
    ).reshape(items, 4, rows, HEAD_DIM)
    if items < ctx_count:
        packed = jnp.pad(packed, ((0, ctx_count - items), (0, 0), (0, 0), (0, 0)))
    arrived = lax.all_to_all(packed, "ctx", 0, 0, tiled=True)
    arrived = jnp.concatenate([arrived, arrived[:G_BLOCKS]], axis=0)
    mine = lax.dynamic_slice_in_dim(arrived, start, G_BLOCKS, 0)
    mine = mine.transpose(1, 0, 2, 3).reshape(4, group, HEAD_DIM)

    item_pos = (start * rows + jnp.arange(group, dtype=jnp.int32)) % seq_total
    item_cos, item_sin = angles(item_pos)
    item_cos = jnp.concatenate([item_cos, item_cos], axis=1)
    item_sin = jnp.concatenate([item_sin, -item_sin], axis=1)
    results = attend(mine[0], mine[1], mine[2], mine[3], item_cos, item_sin)

    results = results.reshape(4, G_BLOCKS, rows, HEAD_DIM).transpose(1, 0, 2, 3)
    back = jnp.concatenate([results] * (ctx_count // G_BLOCKS), axis=0)
    back = jnp.concatenate([back, back], axis=0)
    back = lax.dynamic_slice_in_dim(back, (ctx_count - start) % ctx_count, ctx_count, 0)
    returned = lax.all_to_all(back, "ctx", 0, 0, tiled=True)
    returned = returned[:items].reshape(heads_local, groups, 4, rows, HEAD_DIM)
    my_group = ((ctx_place - local_shift * half_group) % ctx_count) // G_BLOCKS
    chosen = returned[:, 0]
    for other in range(1, groups):
        chosen = jnp.where((my_group == other)[:, None, None, None], returned[:, other], chosen)
    chosen = chosen.transpose(1, 2, 0, 3).reshape(4, rows, width_local)
    context, dq_pre, dk_pre, dv_b = chosen[0], chosen[1], chosen[2], chosen[3]

    partial_value = lax.dot_general(context, whole[3], LAST, preferred_element_type=jnp.float32)
    output = (tokens.astype(jnp.float32) + scatter_head(partial_value)).astype(jnp.bfloat16)

    g_q = jnp.dot(dq_pre, query_up.T, preferred_element_type=jnp.float32)
    g_v = jnp.dot(dv_b, value_up.T, preferred_element_type=jnp.float32)
    g_both = 2.0 * jnp.concatenate([g_q, g_v], axis=1)
    downs = jnp.concatenate([query_down, value_down], axis=1).astype(jnp.float32)
    d_normed = lax.dot_general(dq_pre, whole[0], LAST, preferred_element_type=jnp.float32)
    d_normed += lax.dot_general(dk_pre, whole[1], LAST, preferred_element_type=jnp.float32)
    d_normed += lax.dot_general(dv_b, whole[2], LAST, preferred_element_type=jnp.float32)
    d_normed += lax.dot_general(g_both, downs, LAST, precision=lax.Precision.HIGHEST)
    row_mean = sum_head(jnp.sum(d_normed * xn, axis=-1, keepdims=True)) / full_x.shape[1]
    x_slice = tokens.astype(jnp.float32) * rinv
    grad_tokens = (
        grad_out.astype(jnp.float32) + rinv * (scatter_head(d_normed) - x_slice * row_mean)
    ).astype(jnp.bfloat16)

    scale_out = 1.0 / seq_total**0.5
    down = lax.dot_general(
        g_both, normed.astype(jnp.float32), FIRST, precision=lax.Precision.HIGHEST
    )
    up_q = 2.0 * lax.dot_general(low_q, dq_pre, FIRST, preferred_element_type=jnp.float32)
    up_v = 2.0 * lax.dot_general(low_v, dv_b, FIRST, preferred_element_type=jnp.float32)
    ups = jnp.concatenate([up_q, up_v], axis=0)
    wide = jnp.zeros((2 * rank, head_count * width_local), jnp.float32)
    wide = lax.dynamic_update_slice_in_dim(wide, ups, head_place * width_local, 1)
    total = lax.psum(jnp.concatenate([down, wide], axis=1), ("ctx", "head")) * scale_out
    depth = full_x.shape[1]
    downs_out = total[:, :depth].T
    ups_out = lax.dynamic_slice_in_dim(total, depth + head_place * width_local, width_local, 1)
    return (
        output,
        grad_tokens,
        downs_out[:, :rank],
        ups_out[:rank],
        downs_out[:, rank:],
        ups_out[rank:],
    )


def solution(mesh):
    in_specs = (
        P("ctx", "head"),
        P("ctx", "head"),
        P("ctx", "head"),
        P("ctx", "head"),
        P("head", "ctx"),
        P(),
        P(None, "head"),
        P(),
        P(None, "head"),
        P(),
        P("ctx", "head"),
    )
    out_specs = (P("ctx", "head"), P("ctx", "head"), P(), P(None, "head"), P(), P(None, "head"))
    return jax.shard_map(
        per_device, mesh=mesh, in_specs=in_specs, out_specs=out_specs, check_vma=False
    )
```

time: 1160 us -> 715 us (0.62)
  waiting for transfers between devices: 704 us -> 534 us
  starting transfers between devices: 134 us -> 31.4 us
  matrix products: 159 us -> 57.2 us
  local copies, waits for them, and re-layouts: 97.5 us -> 24.5 us
  Pallas kernels: 0 us -> 14.3 us
    all_to_all x0 -> x2, waiting for transfers between devices: none -> 149 us  [the longest x1 77.3 us: per_device(): returned = lax.all_to_all(back, 'ctx', 0, 0, tiled=True)]
    ppermute x14 -> x5, starting transfers between devices: 134 us -> 6.67 us  [swapped(): return lax.ppermute(value, 'head', [(0, 1), (1, 0)])]
    reduce_scatter x2 -> x0, waiting for transfers between devices: 106 us -> none  [the longest x1 53.8 us: per_device(): mine = lax.psum_scatter(d_normed, 'head', scatter_dimension=1, tiled=True)]
    psum x2 -> x1, waiting for transfers between devices: 207 us -> 109 us  [per_device(): lax.psum(jnp.concatenate([down, wide], axis=1), ('ctx', 'head')) * scale_out]
    dot_general x16 -> x9, matrix products: 125 us -> 33.2 us  [the longest x1 6.52 us: per_device(): jnp.dot(full_dy, whole[3], preferred_element_type=jnp.float32)]
    all_gather x4, waiting for transfers between devices: 318 us -> 235 us  [per_device(): lax.all_gather(w, 'ctx', axis=0, tiled=True)]
    unnamed x77 -> x62, local copies, waits for them, and re-layouts: 47.4 us -> 5.77 us
    ppermute x14 -> x5, waiting for transfers between devices: 70.6 us -> 38.1 us  [swapped(): return lax.ppermute(value, 'head', [(0, 1), (1, 0)])]
  transfers between devices with their start and end apart: 22 -> 12, of which waited for: 12 -> 9; matrix products, arithmetic and copies ran while one was open for 14% -> 9% of each run, Pallas kernels for 0% -> 0%
where the time goes in v1:
time: 715 us; the launch traced here: 706 us
  waiting for transfers between devices  534 us (75%)
  matrix products  57.2 us (8%)
  starting transfers between devices  31.4 us (4%)
  other arithmetic  28.4 us (4%)
  local copies, waits for them, and re-layouts  24.5 us (3%)
  between operations  15.3 us (2%)
  Pallas kernels  14.3 us (2%)
    all_gather x4, waiting for transfers between devices, per_device(): lax.all_gather(w, 'ctx', axis=0, tiled=True)  235 us
    psum x1, waiting for transfers between devices, per_device(): lax.psum(jnp.concatenate([down, wide], axis=1), ('ctx', 'head')) * scale_out  109 us
    all_to_all x1, waiting for transfers between devices, per_device(): returned = lax.all_to_all(back, 'ctx', 0, 0, tiled=True)  77.3 us
    all_to_all x1, waiting for transfers between devices, per_device(): arrived = lax.all_to_all(packed, 'ctx', 0, 0, tiled=True)  71.9 us
    ppermute x5, waiting for transfers between devices, swapped(): return lax.ppermute(value, 'head', [(0, 1), (1, 0)])  38.1 us
    all_to_all x1, starting transfers between devices, per_device(): returned = lax.all_to_all(back, 'ctx', 0, 0, tiled=True)  19.6 us
    pallas_call x1, Pallas kernels, attend(): pl.pallas_call(functools.partial(attend_kernel, 256), out_shape=jax.Shape...  14.3 us
  transfers between devices with their start and end apart: 12, of which 9 were waited for; matrix products, arithmetic and copies ran while one was open for 9% of the time, Pallas kernels for 0%

profile of v1, /device:TPU:0, one launch (start us, length us, event | category | flops | bytes accessed | tf_op | source)
XLA Modules:
  0.0 705.6 jit_solution(5686017016714661204)
XLA Ops:
  10.0 3.0 collective-permute-start
  13.7 23.5 %collective-permute-done = bf16[256,2048]{1,0:T(8,128)(2,1)S(1)} collective-permute-done((bf16[256,2048]{1,0:T(8,128)(2,1)}, bf16[256,2048]{1,0:T(8,128)(2,1)S(1)}, u32[]{:S(2)}, u32[]{:S(2)}) %collective-permute-start) | collective-permute-done | bytes 1048608 | tf_op jit(solution)/shard_map/ppermute | solution.py:38
  44.4 14.6 %collective-permute-done.1 = bf16[256,2048]{1,0:T(8,128)(2,1)} collective-permute-done((bf16[256,2048]{1,0:T(8,128)(2,1)}, bf16[256,2048]{1,0:T(8,128)(2,1)}, u32[]{:S(2)}, u32[]{:S(2)}) %collective-permute-start.1) | collective-permute-done | bytes 1048608 | tf_op jit(solution)/shard_map/ppermute | solution.py:38
  61.6 26.2 %all-gather.5.cloned.1.call-done = bf16[4096,1024]{1,0:T(8,128)(2,1)} async-done(((bf16[256,1024]{1,0:T(8,128)(2,1)}), bf16[4096,1024]{1,0:T(8,128)(2,1)}) %all-gather.5.cloned.1.call-update) | async-done | bytes 8388624 | tf_op jit(solution)/shard_map/all_gather | solution.py:154
  87.8 6.0 fusion.21
  95.0 68.2 %all-gather.7.cloned.1.call-done = bf16[4096,1024]{1,0:T(8,128)(2,1)} async-done(((bf16[256,1024]{1,0:T(8,128)(2,1)}), bf16[4096,1024]{1,0:T(8,128)(2,1)}) %all-gather.7.cloned.1.call-update) | async-done | bytes 8388624 | tf_op jit(solution)/shard_map/all_gather | solution.py:154
  163.1 5.7 convolution_bitcast_fusion
  170.0 68.5 %all-gather.9.cloned.1.call-done = bf16[4096,1024]{1,0:T(8,128)(2,1)} async-done(((bf16[256,1024]{1,0:T(8,128)(2,1)}), bf16[4096,1024]{1,0:T(8,128)(2,1)}) %all-gather.9.cloned.1.call-update) | async-done | bytes 8388624 | tf_op jit(solution)/shard_map/all_gather | solution.py:154
  238.5 5.9 fusion.29
  244.5 72.3 %all-gather.11.cloned.1.call-done = bf16[4096,1024]{0,1:T(8,128)(2,1)} async-done(((bf16[256,1024]{0,1:T(8,128)(2,1)}), bf16[4096,1024]{0,1:T(8,128)(2,1)}) %all-gather.11.cloned.1.call-update) | async-done | bytes 8388624 | tf_op jit(solution)/shard_map/all_gather | solution.py:154
  316.9 6.5 fusion.26
  326.4 3.0 broadcast_in_dim.12
  329.4 4.7 all-to-all-start
  335.4 3.7 multiply_sine_fusion
  339.7 71.9 %all-to-all-done = bf16[16,4,256,128]{3,2,1,0:T(8,128)(2,1)} async-done(((bf16[16,4,256,128]{3,2,1,0:T(8,128)(2,1)}), bf16[16,4,256,128]{3,2,1,0:T(8,128)(2,1)}, u32[]{:S(2)}, u32[]{:S(2)}) %all-to-all-start) | async-done | bytes 4194336 | tf_op jit(solution)/shard_map/all_to_all | solution.py:192
  416.0 14.3 %shard_map.154 = bf16[4,2048,128]{2,1,0:T(8,128)(2,1)} custom-call(bf16[2048,128]{1,0:T(8,128)(2,1)S(1)} %bitcast.95, bf16[2048,128]{1,0:T(8,128)(2,1)S(1)} %bitcast.94, bf16[2048,128]{1,0:T(8,128)(2,1)S(1)} %bitcast.93, bf16[2048,128]{1,0:T(8,128)(2,1)S(1)} %bitcast.92, f32[2048,128]{1,0:T(8,128)S(1)} %get-tuple-element.37.cos_ref, ...), custom_call_target="tpu_custom_call" | custom-call | flops 2684354560 | bytes 8388608 | tf_op jit(solution)/shard_map/pallas_call | solution.py:106
  432.2 4.2 fusion.6
  436.4 19.6 %all-to-all-start.1 = ((bf16[16,4,256,128]{3,2,1,0:T(8,128)(2,1)}), bf16[16,4,256,128]{3,2,1,0:T(8,128)(2,1)}, u32[]{:S(2)}, u32[]{:S(2)}) async-start(bf16[16,4,256,128]{3,2,1,0:T(8,128)(2,1)} %fusion.6), calls=%async_computation.1 | async-start | bytes 8388608 | tf_op jit(solution)/shard_map/all_to_all | solution.py:207
  456.4 77.3 %all-to-all-done.1 = bf16[16,4,256,128]{3,2,1,0:T(8,128)(2,1)} async-done(((bf16[16,4,256,128]{3,2,1,0:T(8,128)(2,1)}), bf16[16,4,256,128]{3,2,1,0:T(8,128)(2,1)}, u32[]{:S(2)}, u32[]{:S(2)}) %all-to-all-start.1) | async-done | bytes 4194336 | tf_op jit(solution)/shard_map/all_to_all | solution.py:207
  549.8 6.1 fusion.59
  555.9 6.0 convolution_add_fusion.2
  572.3 6.0 fusion.58
  581.9 109.4 %all-reduce.2.cloned.1.call-done = f32[16,6144]{1,0:T(8,128)} async-done(((f32[16,6144]{1,0:T(8,128)}), f32[16,6144]{1,0:T(8,128)}) %all-reduce.2.cloned.1.call-update) | async-done | bytes 393232 | tf_op jit(solution)/shard_map/psum | solution.py:242
  693.7 5.1 fusion.12
  (126 shorter events, 58.5 us)
Async XLA Ops:
  7.2 35.9 %copy-start = (bf16[8,1024]{1,0:T(8,128)(2,1)S(1)}, bf16[8,1024]{1,0:T(8,128)(2,1)}, u32[]{:S(2)}) copy-start(bf16[8,1024]{1,0:T(8,128)(2,1)} %param.19) | copy-start | bytes 49156
  7.2 80.6 %all-gather.5.cloned.1.call-start = ((), (), s32[]{:S(2)}) async-start(), calls=%async_computation.2 | async-start | bytes 8912896 | tf_op jit(solution)/shard_map/all_gather | solution.py:154
  7.9 155.2 %all-gather.7.cloned.1.call-start = ((), (), s32[]{:S(2)}) async-start(), calls=%async_computation.3 | async-start | bytes 8912896 | tf_op jit(solution)/shard_map/all_gather | solution.py:154
  8.7 229.8 %all-gather.9.cloned.1.call-start = ((), (), s32[]{:S(2)}) async-start(), calls=%async_computation.4 | async-start | bytes 8912896 | tf_op jit(solution)/shard_map/all_gather | solution.py:154
  9.4 307.5 %all-gather.11.cloned.1.call-start = ((), (), s32[]{:S(2)}) async-start(), calls=%async_computation.5 | async-start | bytes 8912896 | tf_op jit(solution)/shard_map/all_gather | solution.py:154
  10.0 27.2 %collective-permute-start = (bf16[256,2048]{1,0:T(8,128)(2,1)}, bf16[256,2048]{1,0:T(8,128)(2,1)S(1)}, u32[]{:S(2)}, u32[]{:S(2)}) collective-permute-start(bf16[256,2048]{1,0:T(8,128)(2,1)} %param.11), channel_id=1, source_target_pairs={{0,1},{1,0},{2,3},{3,2},{4,5},{5,4},{6,7},{7,6},{8,9},{9,8},{10,11... | collective-permute-start | bytes 3145736 | tf_op jit(solution)/shard_map/ppermute | solution.py:38
  13.0 45.9 %collective-permute-start.1 = (bf16[256,2048]{1,0:T(8,128)(2,1)}, bf16[256,2048]{1,0:T(8,128)(2,1)}, u32[]{:S(2)}, u32[]{:S(2)}) collective-permute-start(bf16[256,2048]{1,0:T(8,128)(2,1)} %param.21), channel_id=1, source_target_pairs={{0,1},{1,0},{2,3},{3,2},{4,5},{5,4},{6,7},{7,6},{8,9},{9,8},{10,11... | collective-permute-start | bytes 3145736 | tf_op jit(solution)/shard_map/ppermute | solution.py:38
  39.8 198.7 %copy-start.1 = (bf16[256,4096]{1,0:T(8,128)(2,1)}, bf16[256,4096]{1,0:T(8,128)(2,1)S(1)}, u32[]{:S(2)}) copy-start(bf16[256,4096]{1,0:T(8,128)(2,1)S(1)} %fusion.1) | copy-start | bytes 6291460
  39.8 19.2 %copy-start.11 = (bf16[256,2048]{1,0:T(8,128)(2,1)S(1)}, bf16[256,2048]{1,0:T(8,128)(2,1)}, u32[]{:S(2)}) copy-start(bf16[256,2048]{1,0:T(8,128)(2,1)} %param.21) | copy-start | bytes 3145732
  316.9 6.6 copy-start.7
  316.9 6.6 copy-start.8
  329.4 82.3 %all-to-all-start = ((bf16[16,4,256,128]{3,2,1,0:T(8,128)(2,1)}), bf16[16,4,256,128]{3,2,1,0:T(8,128)(2,1)}, u32[]{:S(2)}, u32[]{:S(2)}) async-start(bf16[16,4,256,128]{3,2,1,0:T(8,128)(2,1)} %bitcast.96), calls=%async_computation | async-start | bytes 8388608 | tf_op jit(solution)/shard_map/all_to_all | solution.py:192
  436.4 97.3 %all-to-all-start.1 = ((bf16[16,4,256,128]{3,2,1,0:T(8,128)(2,1)}), bf16[16,4,256,128]{3,2,1,0:T(8,128)(2,1)}, u32[]{:S(2)}, u32[]{:S(2)}) async-start(bf16[16,4,256,128]{3,2,1,0:T(8,128)(2,1)} %fusion.6), calls=%async_computation.1 | async-start | bytes 8388608 | tf_op jit(solution)/shard_map/all_to_all | solution.py:207
  456.0 235.2 %all-reduce.2.cloned.1.call-start = ((), (), s32[]{:S(2)}) async-start(), calls=%async_computation.6 | async-start | bytes 786432 | tf_op jit(solution)/shard_map/psum | solution.py:242
  536.2 8.1 %copy-start.17 = (bf16[8,1024]{1,0:T(8,128)(2,1)S(1)}, bf16[8,1024]{1,0:T(8,128)(2,1)}, u32[]{:S(2)}) copy-start(bf16[8,1024]{1,0:T(8,128)(2,1)} %param.17) | copy-start | bytes 49156
  536.2 9.3 %copy-start.19 = (bf16[256,8]{0,1:T(8,128)(2,1)S(1)}, bf16[256,8]{0,1:T(8,128)(2,1)}, u32[]{:S(2)}) copy-start(bf16[256,8]{0,1:T(8,128)(2,1)} %copy-done.18) | copy-start | bytes 12292
  536.3 10.5 %copy-start.2 = (bf16[256,4096]{1,0:T(8,128)(2,1)S(1)}, bf16[256,4096]{1,0:T(8,128)(2,1)}, u32[]{:S(2)}) copy-start(bf16[256,4096]{1,0:T(8,128)(2,1)} %copy-done.1) | copy-start | bytes 6291460
  549.8 12.2 %slice-start = ((s8[8388608]{0:T(1024)(128)(4,1)}), s8[4194304]{0:T(1024)(128)(4,1)S(1)}, s32[]{:S(2)}) async-start(s8[8388608]{0:T(1024)(128)(4,1)} %bitcast.115), calls=%async_computation.7 | async-start | bytes 8388608
  564.5 7.3 %copy-start.13 = (bf16[1,256,8,128]{3,1,0,2:T(8,128)(2,1)S(1)}, bf16[1,256,8,128]{3,1,0,2:T(8,128)(2,1)}, u32[]{:S(2)}) copy-start(bf16[1,256,8,128]{3,1,0,2:T(8,128)(2,1)} %get-tuple-element.9) | copy-start | bytes 1572868
  567.1 14.7 %collective-permute-start.4 = (f32[256,1]{0,1:T(1,128)S(1)}, f32[256,1]{0,1:T(1,128)S(1)}, u32[]{:S(2)}, u32[]{:S(2)}) collective-permute-start(f32[256,1]{0,1:T(1,128)S(1)} %bitcast.113), channel_id=1, source_target_pairs={{0,1},{1,0},{2,3},{3,2},{4,5},{5,4},{6,7},{7,6},{8,9},{9,8},{10,11... | collective-permute-start | bytes 3080 | tf_op jit(solution)/shard_map/ppermute | solution.py:38
  570.3 123.4 %collective-permute-start.3 = (bf16[256,2048]{1,0:T(8,128)(2,1)}, bf16[256,2048]{1,0:T(8,128)(2,1)S(1)}, u32[]{:S(2)}, u32[]{:S(2)}) collective-permute-start(bf16[256,2048]{1,0:T(8,128)(2,1)} %dynamic-slice_convert_fusion), channel_id=1, source_target_pairs={{0,1},{1,0},{2,3},{3,2},{4,5},{5,4},{6,7},{7,6},{8,9},{9,8},{10,11... | collective-permute-start | bytes 3145736 | tf_op jit(solution)/shard_map/ppermute | solution.py:38
  580.2 113.5 %copy-start.10 = (bf16[256,2048]{1,0:T(8,128)(2,1)S(1)}, bf16[256,2048]{1,0:T(8,128)(2,1)}, u32[]{:S(2)}) copy-start(bf16[256,2048]{1,0:T(8,128)(2,1)} %param.11) | copy-start | bytes 3145732
  580.2 113.5 %copy-start.12 = (bf16[256,2048]{1,0:T(8,128)(2,1)S(1)}, bf16[256,2048]{1,0:T(8,128)(2,1)}, u32[]{:S(2)}) copy-start(bf16[256,2048]{1,0:T(8,128)(2,1)} %param.21) | copy-start | bytes 3145732
  581.3 112.3 %collective-permute-start.2 = (bf16[256,2048]{1,0:T(8,128)(2,1)}, bf16[256,2048]{1,0:T(8,128)(2,1)}, u32[]{:S(2)}, u32[]{:S(2)}) collective-permute-start(bf16[256,2048]{1,0:T(8,128)(2,1)} %dynamic-slice_convert_fusion.1), channel_id=1, source_target_pairs={{0,1},{1,0},{2,3},{3,2},{4,5},{5,4},{6,7},{7,6},{8,9},{9,8},{10,11... | collective-permute-start | bytes 3145736 | tf_op jit(solution)/shard_map/ppermute | solution.py:38
  (17 other events, 49.8 us)
Sparse Core Ops, SparseCore 0:
  10.2 77.5 all-gather.4
  90.0 73.1 all-gather.6
  165.3 73.1 all-gather.8
  240.5 76.3 all-gather.10
  548.7 142.5 all-reduce.1

commit v2 on v1

--- a/solution.py
+++ b/solution.py
@@ -121,6 +121,74 @@
     )(query, key, value, d_context, cosine, sine)
 
 
+def rolled(value, begin):
+    count = value.shape[0]
+    return lax.dynamic_slice_in_dim(jnp.concatenate([value, value], axis=0), begin, count, 0)
+
+
+def spread_pairs(packed, turn, item_cos, item_sin):
+    heads, _, rows, _ = packed.shape
+    count = lax.axis_size("ctx")
+    core = lax.axis_index("ctx") % 2
+    even = core == 0
+    pairs = [(place, place ^ 1) for place in range(count)]
+
+    def swap(low, high):
+        kept = jnp.where(even, low, high)
+        return kept, lax.ppermute(jnp.where(even, high, low), "ctx", pairs)
+
+    arrived = lax.all_to_all(packed.reshape(count, 2, rows, HEAD_DIM), "ctx", 0, 0, tiled=True)
+    arrived = rolled(arrived, turn)
+    kept, other = swap(arrived[:G_BLOCKS], arrived[G_BLOCKS:])
+
+    def flat(array):
+        return array.transpose(1, 0, 2, 3).reshape(2, G_BLOCKS * rows, HEAD_DIM)
+
+    kept, other = flat(kept), flat(other)
+    low = jnp.where(even, kept, other)
+    high = jnp.where(even, other, kept)
+    results = attend(low[0], low[1], high[0], high[1], item_cos, item_sin)
+    results = results.reshape(4, G_BLOCKS, rows, HEAD_DIM).transpose(1, 0, 2, 3)
+    kept, other = swap(results[:, :2], results[:, 2:])
+    both = jnp.concatenate([jnp.where(even, kept, other), jnp.where(even, other, kept)], axis=0)
+    returned = lax.all_to_all(rolled(both, (count - turn) % count), "ctx", 0, 0, tiled=True)
+    return returned.reshape(heads, 4, rows, HEAD_DIM)
+
+
+def spread_copies(packed, local_shift, start, items, item_cos, item_sin):
+    heads, _, rows, _ = packed.shape
+    count = lax.axis_size("ctx")
+    groups = items // heads
+    packed = jnp.broadcast_to(packed[:, None], (heads, groups, 4, rows, HEAD_DIM))
+    packed = packed.reshape(items, 4, rows, HEAD_DIM)
+    if items < count:
+        packed = jnp.pad(packed, ((0, count - items), (0, 0), (0, 0), (0, 0)))
+    arrived = lax.all_to_all(packed, "ctx", 0, 0, tiled=True)
+    mine = rolled(arrived, start)[:G_BLOCKS]
+    mine = mine.transpose(1, 0, 2, 3).reshape(4, G_BLOCKS * rows, HEAD_DIM)
+    results = attend(mine[0], mine[1], mine[2], mine[3], item_cos, item_sin)
+    results = results.reshape(4, G_BLOCKS, rows, HEAD_DIM).transpose(1, 0, 2, 3)
+    back = rolled(jnp.concatenate([results] * (count // G_BLOCKS), axis=0), (count - start) % count)
+    returned = lax.all_to_all(back, "ctx", 0, 0, tiled=True)
+    returned = returned[:items].reshape(heads, groups, 4, rows, HEAD_DIM)
+    turn = local_shift * (G_BLOCKS // 2)
+    my_group = ((lax.axis_index("ctx") - turn) % count) // G_BLOCKS
+    chosen = returned[:, 0]
+    for other in range(1, groups):
+        chosen = jnp.where((my_group == other)[:, None, None, None], returned[:, other], chosen)
+    return chosen
+
+
+def sum_ctx(value):
+    count = lax.axis_size("ctx")
+    if value.size % (count * 128) != 0:
+        return lax.psum(value, "ctx")
+    parts = value.reshape(count, value.size // (count * 128), 128)
+    part = jnp.sum(lax.all_to_all(parts, "ctx", 0, 0, tiled=True), axis=0, keepdims=True)
+    whole = lax.all_to_all(jnp.broadcast_to(part, parts.shape), "ctx", 0, 0, tiled=True)
+    return whole.reshape(value.shape)
+
+
 def per_device(
     tokens,
     w_query,
@@ -138,7 +206,6 @@
     slice_width = tokens.shape[1]
     ctx_count = lax.axis_size("ctx")
     ctx_place = lax.axis_index("ctx")
-    head_count = lax.axis_size("head")
     head_place = lax.axis_index("head")
     width_local = w_query.shape[1]
     heads_local = width_local // HEAD_DIM
@@ -150,9 +217,11 @@
     half_group = G_BLOCKS // 2
     rank = query_down.shape[1]
 
-    whole = [
-        lax.all_gather(w, "ctx", axis=0, tiled=True) for w in (w_query, w_key, w_value, w_out.T)
-    ]
+    weights = lax.all_gather(
+        jnp.concatenate([w_query, w_key, w_value, w_out.T], axis=1), "ctx", axis=0, tiled=True
+    )
+    w_qkv = weights[:, : 3 * width_local]
+    w_out_t = weights[:, 3 * width_local :]
 
     full_x = gather_head(tokens)
     full_dy = gather_head(grad_out)
@@ -164,9 +233,8 @@
     low_v = jnp.dot(normed, value_down, preferred_element_type=jnp.float32).astype(jnp.bfloat16)
     positions = ctx_place * rows + jnp.arange(rows, dtype=jnp.int32)
     cosine, sine = angles(positions)
-    q_lin = jnp.dot(normed, whole[0], preferred_element_type=jnp.float32)
-    k_lin = jnp.dot(normed, whole[1], preferred_element_type=jnp.float32)
-    v_lin = jnp.dot(normed, whole[2], preferred_element_type=jnp.float32)
+    linear = jnp.dot(normed, w_qkv, preferred_element_type=jnp.float32)
+    q_lin, k_lin, v_lin = jnp.split(linear, 3, axis=1)
     query = rope(
         q_lin + 2.0 * jnp.dot(low_q, query_up, preferred_element_type=jnp.float32), cosine, sine
     ).astype(jnp.bfloat16)
@@ -174,55 +242,35 @@
     value = (v_lin + 2.0 * jnp.dot(low_v, value_up, preferred_element_type=jnp.float32)).astype(
         jnp.bfloat16
     )
-    d_context = jnp.dot(full_dy, whole[3], preferred_element_type=jnp.float32).astype(jnp.bfloat16)
+    d_context = jnp.dot(full_dy, w_out_t, preferred_element_type=jnp.float32).astype(jnp.bfloat16)
 
     local_shift = lax.dynamic_slice_in_dim(shifted, head_place * heads_local, heads_local)
     item = jnp.minimum(ctx_place, items - 1)
-    item_group = item % groups
     item_shift = lax.dynamic_index_in_dim(local_shift, item // groups, keepdims=False)
-    start = (item_group * G_BLOCKS + item_shift * half_group) % ctx_count
-
-    packed = jnp.stack([query, key, value, d_context])
-    packed = packed.reshape(4, rows, heads_local, HEAD_DIM).transpose(2, 0, 1, 3)
-    packed = jnp.broadcast_to(
-        packed[:, None], (heads_local, groups, 4, rows, HEAD_DIM)
-    ).reshape(items, 4, rows, HEAD_DIM)
-    if items < ctx_count:
-        packed = jnp.pad(packed, ((0, ctx_count - items), (0, 0), (0, 0), (0, 0)))
-    arrived = lax.all_to_all(packed, "ctx", 0, 0, tiled=True)
-    arrived = jnp.concatenate([arrived, arrived[:G_BLOCKS]], axis=0)
-    mine = lax.dynamic_slice_in_dim(arrived, start, G_BLOCKS, 0)
-    mine = mine.transpose(1, 0, 2, 3).reshape(4, group, HEAD_DIM)
-
+    start = (item % groups * G_BLOCKS + item_shift * half_group) % ctx_count
     item_pos = (start * rows + jnp.arange(group, dtype=jnp.int32)) % seq_total
     item_cos, item_sin = angles(item_pos)
     item_cos = jnp.concatenate([item_cos, item_cos], axis=1)
     item_sin = jnp.concatenate([item_sin, -item_sin], axis=1)
-    results = attend(mine[0], mine[1], mine[2], mine[3], item_cos, item_sin)
-
-    results = results.reshape(4, G_BLOCKS, rows, HEAD_DIM).transpose(1, 0, 2, 3)
-    back = jnp.concatenate([results] * (ctx_count // G_BLOCKS), axis=0)
-    back = jnp.concatenate([back, back], axis=0)
-    back = lax.dynamic_slice_in_dim(back, (ctx_count - start) % ctx_count, ctx_count, 0)
-    returned = lax.all_to_all(back, "ctx", 0, 0, tiled=True)
-    returned = returned[:items].reshape(heads_local, groups, 4, rows, HEAD_DIM)
-    my_group = ((ctx_place - local_shift * half_group) % ctx_count) // G_BLOCKS
-    chosen = returned[:, 0]
-    for other in range(1, groups):
-        chosen = jnp.where((my_group == other)[:, None, None, None], returned[:, other], chosen)
+
+    packed = jnp.stack([query, key, value, d_context])
+    packed = packed.reshape(4, rows, heads_local, HEAD_DIM).transpose(2, 0, 1, 3)
+    if groups == 2 and items == ctx_count:
+        chosen = spread_pairs(packed, item_shift * half_group, item_cos, item_sin)
+    else:
+        chosen = spread_copies(packed, local_shift, start, items, item_cos, item_sin)
     chosen = chosen.transpose(1, 2, 0, 3).reshape(4, rows, width_local)
     context, dq_pre, dk_pre, dv_b = chosen[0], chosen[1], chosen[2], chosen[3]
 
-    partial_value = lax.dot_general(context, whole[3], LAST, preferred_element_type=jnp.float32)
+    partial_value = lax.dot_general(context, w_out_t, LAST, preferred_element_type=jnp.float32)
     output = (tokens.astype(jnp.float32) + scatter_head(partial_value)).astype(jnp.bfloat16)
 
     g_q = jnp.dot(dq_pre, query_up.T, preferred_element_type=jnp.float32)
     g_v = jnp.dot(dv_b, value_up.T, preferred_element_type=jnp.float32)
     g_both = 2.0 * jnp.concatenate([g_q, g_v], axis=1)
     downs = jnp.concatenate([query_down, value_down], axis=1).astype(jnp.float32)
-    d_normed = lax.dot_general(dq_pre, whole[0], LAST, preferred_element_type=jnp.float32)
-    d_normed += lax.dot_general(dk_pre, whole[1], LAST, preferred_element_type=jnp.float32)
-    d_normed += lax.dot_general(dv_b, whole[2], LAST, preferred_element_type=jnp.float32)
+    grads = jnp.concatenate([dq_pre, dk_pre, dv_b], axis=1)
+    d_normed = lax.dot_general(grads, w_qkv, LAST, preferred_element_type=jnp.float32)
     d_normed += lax.dot_general(g_both, downs, LAST, precision=lax.Precision.HIGHEST)
     row_mean = sum_head(jnp.sum(d_normed * xn, axis=-1, keepdims=True)) / full_x.shape[1]
     x_slice = tokens.astype(jnp.float32) * rinv
@@ -237,12 +285,10 @@
     up_q = 2.0 * lax.dot_general(low_q, dq_pre, FIRST, preferred_element_type=jnp.float32)
     up_v = 2.0 * lax.dot_general(low_v, dv_b, FIRST, preferred_element_type=jnp.float32)
     ups = jnp.concatenate([up_q, up_v], axis=0)
-    wide = jnp.zeros((2 * rank, head_count * width_local), jnp.float32)
-    wide = lax.dynamic_update_slice_in_dim(wide, ups, head_place * width_local, 1)
-    total = lax.psum(jnp.concatenate([down, wide], axis=1), ("ctx", "head")) * scale_out
+    total = sum_ctx(jnp.concatenate([sum_head(down), ups], axis=1)) * scale_out
     depth = full_x.shape[1]
     downs_out = total[:, :depth].T
-    ups_out = lax.dynamic_slice_in_dim(total, depth + head_place * width_local, width_local, 1)
+    ups_out = total[:, depth:]
     return (
         output,
         grad_tokens,

time: 715 us -> 480 us (0.67)
  waiting for transfers between devices: 534 us -> 288 us
  starting transfers between devices: 31.4 us -> 39.6 us
  local copies, waits for them, and re-layouts: 24.5 us -> 31.8 us
    all_gather x4 -> x1, waiting for transfers between devices: 235 us -> 124 us  [per_device(): lax.all_gather(jnp.concatenate([w_query, w_key, w_value, w_out.T], axis=1...]
    psum x1 -> x0, waiting for transfers between devices: 109 us -> none  [per_device(): lax.psum(jnp.concatenate([down, wide], axis=1), ('ctx', 'head')) * scale_out]
    all_to_all x2 -> x4, waiting for transfers between devices: 149 us -> 95.6 us  [the longest x1 41.1 us: spread_pairs(): lax.all_to_all(rolled(both, (count - turn) % count), 'ctx', 0, 0, tiled=T...]
    ppermute x5 -> x6, waiting for transfers between devices: 38.1 us -> 64.7 us  [swapped(): return lax.ppermute(value, 'head', [(0, 1), (1, 0)])]
    unnamed x62 -> x74, local copies, waits for them, and re-layouts: 5.77 us -> 14.1 us
    dot_general x8 -> x4, matrix products: 44.6 us -> 37.5 us  [the longest x1 13 us: per_device(): linear = jnp.dot(normed, w_qkv, preferred_element_type=jnp.float32)]
    all_to_all x2 -> x4, starting transfers between devices: 24.3 us -> 30.4 us  [the longest x1 11.2 us: sum_ctx(): lax.all_to_all(parts, 'ctx', 0, 0, tiled=True)]
  transfers between devices with their start and end apart: 12 -> 13, of which waited for: 9 -> 9; matrix products, arithmetic and copies ran while one was open for 9% -> 6% of each run, Pallas kernels for 0% -> 0%
where the time goes in v2:
time: 480 us; the launch traced here: 473 us
  waiting for transfers between devices  288 us (60%)
  matrix products  53.1 us (11%)
  starting transfers between devices  39.6 us (8%)
  local copies, waits for them, and re-layouts  31.8 us (7%)
  other arithmetic  31.2 us (6%)
  between operations  15.5 us (3%)
  Pallas kernels  14.6 us (3%)
    all_gather x1, waiting for transfers between devices, per_device(): lax.all_gather(jnp.concatenate([w_query, w_key, w_value, w_out.T], axis=1...  124 us
    ppermute x6, waiting for transfers between devices, swapped(): return lax.ppermute(value, 'head', [(0, 1), (1, 0)])  64.7 us
    all_to_all x1, waiting for transfers between devices, spread_pairs(): lax.all_to_all(rolled(both, (count - turn) % count), 'ctx', 0, 0, tiled=T...  41.1 us
    all_to_all x1, waiting for transfers between devices, spread_pairs(): lax.all_to_all(packed.reshape(count, 2, rows, HEAD_DIM), 'ctx', 0, 0, til...  39.5 us
    pallas_call x1, Pallas kernels, attend(): pl.pallas_call(functools.partial(attend_kernel, 256), out_shape=jax.Shape...  14.6 us
    unnamed x74, local copies, waits for them, and re-layouts  14.1 us
    dot_general x1, matrix products, per_device(): linear = jnp.dot(normed, w_qkv, preferred_element_type=jnp.float32)  13 us
    dot_general x1, matrix products, per_device(): lax.dot_general(grads, w_qkv, LAST, preferred_element_type=jnp.float32)  12.1 us
  transfers between devices with their start and end apart: 13, of which 9 were waited for; matrix products, arithmetic and copies ran while one was open for 6% of the time, Pallas kernels for 0%

profile of v2, /device:TPU:0, one launch (start us, length us, event | category | flops | bytes accessed | tf_op | source)
XLA Modules:
  0.0 473.4 jit_solution(4980082183414194311)
XLA Ops:
  14.6 3.0 collective-permute-start.1
  18.3 23.3 %collective-permute-done.1 = bf16[256,2048]{1,0:T(8,128)(2,1)S(1)} collective-permute-done((bf16[256,2048]{1,0:T(8,128)(2,1)S(1)}, bf16[256,2048]{1,0:T(8,128)(2,1)S(1)}, u32[]{:S(2)}, u32[]{:S(2)}) %collective-permute-start.1) | collective-permute-done | bytes 1048608 | tf_op jit(solution)/shard_map/ppermute | solution.py:38
  42.6 20.8 %collective-permute-done = bf16[256,2048]{1,0:T(8,128)(2,1)} collective-permute-done((bf16[256,2048]{1,0:T(8,128)(2,1)S(1)}, bf16[256,2048]{1,0:T(8,128)(2,1)}, u32[]{:S(2)}, u32[]{:S(2)}) %collective-permute-start) | collective-permute-done | bytes 1048608 | tf_op jit(solution)/shard_map/ppermute | solution.py:38
  63.4 3.1 broadcast_select_fusion.1
  70.2 124.3 %all-gather.2.cloned.1.call-done = bf16[4096,4096]{0,1:T(8,128)(2,1)} async-done(((bf16[256,4096]{0,1:T(8,128)(2,1)}), bf16[4096,4096]{0,1:T(8,128)(2,1)}) %all-gather.2.cloned.1.call-update) | async-done | bytes 33554448 | tf_op jit(solution)/shard_map/all_gather | solution.py:220
  194.4 6.4 %fusion.35 = bf16[32,8,8,128]{3,1,2,0:T(8,128)(2,1)S(1)} fusion(bf16[4096,4096]{0,1:T(8,128)(2,1)} %all-gather.2.cloned.1.call-done, bf16[256,2048]{1,0:T(8,128)(2,1)} %get-tuple-element.21, bf16[256,2048]{1,0:T(8,128)(2,1)} %get-tuple-element.20), kind=kOutput, calls=%fused_computation.52 | convolution fusion | flops 2151940096 | bytes 11010048 | tf_op jit(solution)/shard_map/dot_general | solution.py:245
  201.8 13.0 %fusion.2 = f32[256,3072]{1,0:T(8,128)} fusion(bf16[256,4096]{1,0:T(8,128)(2,1)S(1)} %fusion.9, bf16[4096,4096]{0,1:T(8,128)(2,1)} %all-gather.2.cloned.1.call-done), kind=kOutput, calls=%fused_computation.2 | convolution fusion | flops 6442450944 | bytes 30408704 | tf_op jit(solution)/shard_map/dot_general | solution.py:236
  223.5 4.8 %all-to-all-start = ((bf16[16,2,256,128]{3,2,1,0:T(8,128)(2,1)}), bf16[16,2,256,128]{3,2,1,0:T(8,128)(2,1)}, u32[]{:S(2)}, u32[]{:S(2)}) async-start(bf16[16,2,256,128]{3,2,1,0:T(8,128)(2,1)} %bitcast.88), calls=%async_computation | async-start | bytes 4194304 | tf_op jit(solution)/shard_map/all_to_all | solution.py:140
  229.7 39.5 %all-to-all-done = bf16[16,2,256,128]{3,2,1,0:T(8,128)(2,1)} async-done(((bf16[16,2,256,128]{3,2,1,0:T(8,128)(2,1)}), bf16[16,2,256,128]{3,2,1,0:T(8,128)(2,1)}, u32[]{:S(2)}, u32[]{:S(2)}) %all-to-all-start) | async-done | bytes 2097184 | tf_op jit(solution)/shard_map/all_to_all | solution.py:140
  274.7 3.7 multiply_sine_fusion
  281.6 14.6 %shard_map.154 = bf16[4,2048,128]{2,1,0:T(8,128)(2,1)} custom-call(bf16[2048,128]{1,0:T(8,128)(2,1)S(1)} %bitcast.81, bf16[2048,128]{1,0:T(8,128)(2,1)S(1)} %bitcast.80, bf16[2048,128]{1,0:T(8,128)(2,1)S(1)} %bitcast.83, bf16[2048,128]{1,0:T(8,128)(2,1)S(1)} %bitcast.82, f32[2048,128]{1,0:T(8,128)S(1)} %get-tuple-element.47.cos_ref, ...), custom_call_target="tpu_custom_call" | custom-call | flops 2684354560 | bytes 8388608 | tf_op jit(solution)/shard_map/pallas_call | solution.py:106
  300.4 3.0 collective-permute-done.3
  308.2 10.9 %all-to-all-start.1 = ((bf16[16,2,256,128]{3,2,1,0:T(8,128)(2,1)}), bf16[16,2,256,128]{3,2,1,0:T(8,128)(2,1)}, u32[]{:S(2)}, u32[]{:S(2)}) async-start(bf16[16,2,256,128]{3,2,1,0:T(8,128)(2,1)} %fusion.20), calls=%async_computation.1 | async-start | bytes 4194304 | tf_op jit(solution)/shard_map/all_to_all | solution.py:154
  319.1 41.1 %all-to-all-done.1 = bf16[16,2,256,128]{3,2,1,0:T(8,128)(2,1)} async-done(((bf16[16,2,256,128]{3,2,1,0:T(8,128)(2,1)}), bf16[16,2,256,128]{3,2,1,0:T(8,128)(2,1)}, u32[]{:S(2)}, u32[]{:S(2)}) %all-to-all-start.1) | async-done | bytes 2097184 | tf_op jit(solution)/shard_map/all_to_all | solution.py:154
  360.2 2.9 fusion.66
  375.9 12.1 %fusion = f32[256,4096]{1,0:T(8,128)S(1)} fusion(bf16[4096,4096]{0,1:T(8,128)(2,1)} %all-gather.2.cloned.1.call-done, bf16[256,1024]{0,1:T(8,128)(2,1)} %bitcast.94, bf16[256,1024]{0,1:T(8,128)(2,1)} %bitcast.101, bf16[256,1024]{0,1:T(8,128)(2,1)} %bitcast.90), kind=kOutput, calls=%fused_computation | convolution fusion | flops 6447169536 | bytes 30932992 | tf_op jit(solution)/shard_map/dot_general | solution.py:273
  388.1 3.2 fusion.10
  396.8 6.0 %fusion.4 = f32[256,4096]{1,0:T(8,128)S(1)} fusion(bf16[256,1024]{0,1:T(8,128)(2,1)S(1)} %bitcast.102, bf16[4096,4096]{0,1:T(8,128)(2,1)} %all-gather.2.cloned.1.call-done), kind=kOutput, calls=%fused_computation.4 | convolution fusion | flops 2147483648 | bytes 13107200 | tf_op jit(solution)/shard_map/dot_general | solution.py:265
  405.8 20.6 %collective-permute-done.7 = f32[16,4096]{1,0:T(8,128)S(1)} collective-permute-done((f32[16,4096]{1,0:T(8,128)S(1)}, f32[16,4096]{1,0:T(8,128)S(1)}, u32[]{:S(2)}, u32[]{:S(2)}) %collective-permute-start.7) | collective-permute-done | bytes 262176 | tf_op jit(solution)/shard_map/ppermute | solution.py:38
  427.3 11.2 %all-to-all-start.2 = ((f32[16,40,128]{2,1,0:T(8,128)}), f32[16,40,128]{2,1,0:T(8,128)S(1)}, u32[]{:S(2)}, u32[]{:S(2)}) async-start(f32[16,40,128]{2,1,0:T(8,128)} %bitcast.41), calls=%async_computation.2 | async-start | bytes 655360 | tf_op jit(solution)/shard_map/all_to_all | solution.py:187
  440.1 9.5 %all-to-all-done.2 = f32[16,40,128]{2,1,0:T(8,128)S(1)} async-done(((f32[16,40,128]{2,1,0:T(8,128)}), f32[16,40,128]{2,1,0:T(8,128)S(1)}, u32[]{:S(2)}, u32[]{:S(2)}) %all-to-all-start.2) | async-done | bytes 327712 | tf_op jit(solution)/shard_map/all_to_all | solution.py:187
  450.3 3.5 all-to-all-start.3
  453.9 5.5 %fusion.17 = (bf16[256,2048]{1,0:T(8,128)(2,1)}, bf16[256,2048]{1,0:T(8,128)(2,1)}) fusion(bf16[256,2048]{1,0:T(8,128)(2,1)S(1)} %copy-done.9, bf16[256,2048]{1,0:T(8,128)(2,1)} %collective-permute-done.5, f32[256,4096]{1,0:T(8,128)} %copy-done.6, s32[]{:T(128)S(6)} %select_n.152, bf16[256,2048]{1,0:T(8,128)(2,1)S(1)} %copy-done.11, f32[256]{0:T(256)S(1)} %bitcast.106, ...), kind=kLoop, calls=%fused_computation.28 | loop fusion | flops 7340032 | bytes 10487812 | tf_op jit(solution)/shard_map/convert_element_type | solution.py:279
  459.5 5.5 %all-to-all-done.3 = f32[16,40,128]{2,1,0:T(8,128)S(1)} async-done(((f32[16,40,128]{2,1,0:T(8,128)}), f32[16,40,128]{2,1,0:T(8,128)S(1)}, u32[]{:S(2)}, u32[]{:S(2)}) %all-to-all-start.3) | async-done | bytes 327712 | tf_op jit(solution)/shard_map/all_to_all | solution.py:188
  (137 shorter events, 66.4 us)
Async XLA Ops:
  7.2 209.0 %copy-start = (bf16[8,1024]{1,0:T(8,128)(2,1)S(1)}, bf16[8,1024]{1,0:T(8,128)(2,1)}, u32[]{:S(2)}) copy-start(bf16[8,1024]{1,0:T(8,128)(2,1)} %param.19) | copy-start | bytes 49156
  7.2 187.2 %all-gather.2.cloned.1.call-start = ((), (), s32[]{:S(2)}) async-start(), calls=%async_computation.4 | async-start | bytes 35651584 | tf_op jit(solution)/shard_map/all_gather | solution.py:220
  14.6 27.0 %collective-permute-start.1 = (bf16[256,2048]{1,0:T(8,128)(2,1)S(1)}, bf16[256,2048]{1,0:T(8,128)(2,1)S(1)}, u32[]{:S(2)}, u32[]{:S(2)}) collective-permute-start(bf16[256,2048]{1,0:T(8,128)(2,1)S(1)} %copy-done.10), channel_id=1, source_target_pairs={{0,1},{1,0},{2,3},{3,2},{4,5},{5,4},{6,7},{7,6},{8,9},{9,8},{10,11... | collective-permute-start | bytes 3145736 | tf_op jit(solution)/shard_map/ppermute | solution.py:38
  17.6 45.7 %collective-permute-start = (bf16[256,2048]{1,0:T(8,128)(2,1)S(1)}, bf16[256,2048]{1,0:T(8,128)(2,1)}, u32[]{:S(2)}, u32[]{:S(2)}) collective-permute-start(bf16[256,2048]{1,0:T(8,128)(2,1)S(1)} %copy-done.8), channel_id=1, source_target_pairs={{0,1},{1,0},{2,3},{3,2},{4,5},{5,4},{6,7},{7,6},{8,9},{9,8},{10,11... | collective-permute-start | bytes 3145736 | tf_op jit(solution)/shard_map/ppermute | solution.py:38
  17.7 23.9 %copy-start.29 = (f32[64]{0:T(128)}, f32[64]{0:T(128)S(1)}, u32[]{:S(2)}) copy-start(f32[64]{0:T(128)S(1)} %multiply_power_fusion) | copy-start | bytes 772
  223.5 45.7 %all-to-all-start = ((bf16[16,2,256,128]{3,2,1,0:T(8,128)(2,1)}), bf16[16,2,256,128]{3,2,1,0:T(8,128)(2,1)}, u32[]{:S(2)}, u32[]{:S(2)}) async-start(bf16[16,2,256,128]{3,2,1,0:T(8,128)(2,1)} %bitcast.88), calls=%async_computation | async-start | bytes 4194304 | tf_op jit(solution)/shard_map/all_to_all | solution.py:140
  229.6 45.1 %copy-start.30 = (f32[64]{0:T(128)S(1)}, f32[64]{0:T(128)}, u32[]{:S(2)}) copy-start(f32[64]{0:T(128)} %copy-done.29) | copy-start | bytes 772
  273.9 5.1 %collective-permute-start.2 = (bf16[8,2,256,128]{3,2,1,0:T(8,128)(2,1)}, bf16[8,2,256,128]{3,2,1,0:T(8,128)(2,1)}, u32[]{:S(2)}, u32[]{:S(2)}) collective-permute-start(bf16[8,2,256,128]{3,2,1,0:T(8,128)(2,1)} %broadcast_select_fusion.8), channel_id=1, source_target_pairs={{0,2},{2,0},{4,6},{6,4},{8,10},{10,8},{12,14},{14,12},{16,18},{18,... | collective-permute-start | bytes 3145736 | tf_op jit(solution)/shard_map/ppermute | solution.py:138
  300.4 3.0 collective-permute-start.3
  308.2 52.0 %all-to-all-start.1 = ((bf16[16,2,256,128]{3,2,1,0:T(8,128)(2,1)}), bf16[16,2,256,128]{3,2,1,0:T(8,128)(2,1)}, u32[]{:S(2)}, u32[]{:S(2)}) async-start(bf16[16,2,256,128]{3,2,1,0:T(8,128)(2,1)} %fusion.20), calls=%async_computation.1 | async-start | bytes 4194304 | tf_op jit(solution)/shard_map/all_to_all | solution.py:154
  319.1 47.9 %copy-start.24 = (bf16[256,8]{0,1:T(8,128)(2,1)S(1)}, bf16[256,8]{0,1:T(8,128)(2,1)}, u32[]{:S(2)}) copy-start(bf16[256,8]{0,1:T(8,128)(2,1)} %convolution_convert_fusion) | copy-start | bytes 12292
  375.9 12.2 %copy-start.19 = (f32[256,8]{0,1:T(8,128)S(1)}, f32[256,8]{0,1:T(8,128)}, u32[]{:S(2)}) copy-start(f32[256,8]{0,1:T(8,128)} %fusion.74) | copy-start | bytes 24580
  375.9 12.2 %copy-start.26 = (f32[256]{0:T(256)S(1)}, f32[256]{0:T(256)}, u32[]{:S(2)}) copy-start(f32[256]{0:T(256)} %copy-done.25) | copy-start | bytes 3076
  394.5 59.4 %collective-permute-start.5 = (bf16[256,2048]{1,0:T(8,128)(2,1)}, bf16[256,2048]{1,0:T(8,128)(2,1)}, u32[]{:S(2)}, u32[]{:S(2)}) collective-permute-start(bf16[256,2048]{1,0:T(8,128)(2,1)} %dynamic-slice_convert_fusion), channel_id=1, source_target_pairs={{0,1},{1,0},{2,3},{3,2},{4,5},{5,4},{6,7},{7,6},{8,9},{9,8},{10,11... | collective-permute-start | bytes 3145736 | tf_op jit(solution)/shard_map/ppermute | solution.py:38
  396.3 30.1 %collective-permute-start.7 = (f32[16,4096]{1,0:T(8,128)S(1)}, f32[16,4096]{1,0:T(8,128)S(1)}, u32[]{:S(2)}, u32[]{:S(2)}) collective-permute-start(f32[16,4096]{1,0:T(8,128)S(1)} %fusion.51), channel_id=1, source_target_pairs={{0,1},{1,0},{2,3},{3,2},{4,5},{5,4},{6,7},{7,6},{8,9},{9,8},{10,11... | collective-permute-start | bytes 786440 | tf_op jit(solution)/shard_map/ppermute | solution.py:38
  402.8 23.6 %copy-start.18 = (f32[8,1024]{1,0:T(8,128)S(1)}, f32[8,1024]{1,0:T(8,128)}, u32[]{:S(2)}) copy-start(f32[8,1024]{1,0:T(8,128)} %convolution_multiply_fusion.2) | copy-start | bytes 98308
  402.8 35.6 %copy-start.28 = (f32[256]{0:T(256)S(1)}, f32[256]{0:T(256)}, u32[]{:S(2)}) copy-start(f32[256]{0:T(256)} %get-tuple-element.43) | copy-start | bytes 3076
  402.9 51.1 %copy-start.9 = (bf16[256,2048]{1,0:T(8,128)(2,1)S(1)}, bf16[256,2048]{1,0:T(8,128)(2,1)}, u32[]{:S(2)}) copy-start(bf16[256,2048]{1,0:T(8,128)(2,1)} %param.11) | copy-start | bytes 3145732
  402.9 51.1 %copy-start.11 = (bf16[256,2048]{1,0:T(8,128)(2,1)S(1)}, bf16[256,2048]{1,0:T(8,128)(2,1)}, u32[]{:S(2)}) copy-start(bf16[256,2048]{1,0:T(8,128)(2,1)} %param.21) | copy-start | bytes 3145732
  402.9 51.0 %copy-start.27 = (f32[256]{0:T(256)S(1)}, f32[256]{0:T(256)}, u32[]{:S(2)}) copy-start(f32[256]{0:T(256)} %copy-done.25) | copy-start | bytes 3076
  404.0 49.9 %collective-permute-start.4 = (bf16[256,2048]{1,0:T(8,128)(2,1)}, bf16[256,2048]{1,0:T(8,128)(2,1)}, u32[]{:S(2)}, u32[]{:S(2)}) collective-permute-start(bf16[256,2048]{1,0:T(8,128)(2,1)} %dynamic-slice_convert_fusion.1), channel_id=1, source_target_pairs={{0,1},{1,0},{2,3},{3,2},{4,5},{5,4},{6,7},{7,6},{8,9},{9,8},{10,11... | collective-permute-start | bytes 3145736 | tf_op jit(solution)/shard_map/ppermute | solution.py:38
  427.3 22.3 %all-to-all-start.2 = ((f32[16,40,128]{2,1,0:T(8,128)}), f32[16,40,128]{2,1,0:T(8,128)S(1)}, u32[]{:S(2)}, u32[]{:S(2)}) async-start(f32[16,40,128]{2,1,0:T(8,128)} %bitcast.41), calls=%async_computation.2 | async-start | bytes 655360 | tf_op jit(solution)/shard_map/all_to_all | solution.py:187
  438.4 15.4 %collective-permute-start.6 = (f32[256,1]{0,1:T(1,128)S(1)}, f32[256,1]{0,1:T(1,128)S(1)}, u32[]{:S(2)}, u32[]{:S(2)}) collective-permute-start(f32[256,1]{0,1:T(1,128)S(1)} %bitcast.104), channel_id=1, source_target_pairs={{0,1},{1,0},{2,3},{3,2},{4,5},{5,4},{6,7},{7,6},{8,9},{9,8},{10,11... | collective-permute-start | bytes 3080 | tf_op jit(solution)/shard_map/ppermute | solution.py:38
  450.3 14.6 %all-to-all-start.3 = ((f32[16,40,128]{2,1,0:T(8,128)}), f32[16,40,128]{2,1,0:T(8,128)S(1)}, u32[]{:S(2)}, u32[]{:S(2)}) async-start(f32[16,40,128]{2,1,0:T(8,128)} %broadcast_in_dim.5), calls=%async_computation.3 | async-start | bytes 655360 | tf_op jit(solution)/shard_map/all_to_all | solution.py:188
  (21 other events, 84.8 us)
Sparse Core Ops, SparseCore 0:
  14.7 179.6 all-gather.1
